TPU v7x, 32 devices: a whole 2x2x4 slice. The times are simulated.
32 devices in a mesh: ctx: 8 (over z, x), head: 4 (over y, core).
Axes of the slice: x: 2, y: 2, z: 4, core: 2. Of those that a mesh axis runs over, the one named last changes fastest.
Arguments:
- query: bfloat16 [16384, 4096], P(('ctx', 'head')), may hold values from -6 to 6
- key: bfloat16 [16384, 2048], P(('ctx', 'head')), may hold values from -6 to 6
- value: bfloat16 [16384, 2048], P(('ctx', 'head')), may hold values from -6 to 6
- out_grad: bfloat16 [16384, 4096], P(('ctx', 'head')), may hold values from -6 to 6
- block_mask: int32 [128, 9], replicated, may hold values from 0 to 1, as said below
Outputs:
- query_grad: bfloat16 [16384, 4096], P(('ctx', 'head'))
- key_grad: bfloat16 [16384, 2048], P(('ctx', 'head'))
- value_grad: bfloat16 [16384, 2048], P(('ctx', 'head'))
Inputs may be any that keep to these rules, and one draw needn't show every extreme that they name: block_mask[b, 0] is 1 for every block b; block_mask[b, o] = 1 lets query block b attend key block b - o.
All inputs are finite; a program needn't handle non-finite values.
Results may differ from a plain program's by a relative error of at most 0.0095.
Values may be sent and summed in bfloat16 or wider, within the bound.
No kernel may reach another device: no remote copies, remote signals or barrier semaphores. Data moves between devices by JAX's collectives and lax.ppermute only.
A program may use at most 128 MiB of HBM per device.

v0:
```python
import jax
import jax.numpy as jnp
from jax import lax
from jax.sharding import PartitionSpec as P

HEAD_WIDTH = 128
WINDOW = 1024
BLOCK = 128


PRE_SCALE = 168.0 ** (-0.5)


def shifted(block, axis, distance):
    devices = range(lax.axis_size(axis))
    route = [(i - distance, i) for i in devices if i - distance in devices]
    return lax.ppermute(block, axis, route)


def allowed_mask(mask_rows, n_query, n_key, key_lead, key_first):
    q_index = lax.broadcasted_iota(jnp.int32, (n_query, n_key), 0)
    k_index = lax.broadcasted_iota(jnp.int32, (n_query, n_key), 1)
    gap = key_lead + q_index - k_index
    inside = (gap >= 0) & (gap < WINDOW) & (key_first + k_index >= 0)
    q_blocks = n_query // BLOCK
    k_blocks = n_key // BLOCK
    offsets = mask_rows.shape[1]
    a_index = lax.broadcasted_iota(jnp.int32, (q_blocks, k_blocks, offsets), 0)
    b_index = lax.broadcasted_iota(jnp.int32, (q_blocks, k_blocks, offsets), 1)
    o_index = lax.broadcasted_iota(jnp.int32, (q_blocks, k_blocks, offsets), 2)
    picked = jnp.where(o_index == a_index - b_index + key_lead // BLOCK, mask_rows[:, None, :], 0)
    active = jnp.sum(picked, axis=2) > 0
    active = jnp.repeat(jnp.repeat(active, BLOCK, axis=0), BLOCK, axis=1)
    return inside & active


def scores_of(q_part, k_part, allowed):
    n_query = q_part.shape[0]
    n_key = k_part.shape[0]
    kv_groups = k_part.shape[1] // HEAD_WIDTH
    q_heads = q_part.reshape(n_query, kv_groups, -1, HEAD_WIDTH)
    k_heads = k_part.reshape(n_key, kv_groups, HEAD_WIDTH)
    raw_scores = (
        jnp.einsum("qgrd,kgd->grqk", q_heads, k_heads, preferred_element_type=jnp.float32)
        * PRE_SCALE
    )
    return jnp.where(allowed, raw_scores, -jnp.inf)


def grads_from(probs, q_part, g_part, k_part, v_part, delta, want_query):
    n_query = q_part.shape[0]
    n_key = k_part.shape[0]
    kv_groups = k_part.shape[1] // HEAD_WIDTH
    q_heads = q_part.reshape(n_query, kv_groups, -1, HEAD_WIDTH)
    g_heads = g_part.reshape(n_query, kv_groups, -1, HEAD_WIDTH)
    k_heads = k_part.reshape(n_key, kv_groups, HEAD_WIDTH)
    v_heads = v_part.reshape(n_key, kv_groups, HEAD_WIDTH)
    d_value = jnp.einsum(
        "grqk,qgrd->kgd", probs.astype(jnp.bfloat16), g_heads, preferred_element_type=jnp.float32
    )
    d_probs = jnp.einsum("qgrd,kgd->grqk", g_heads, v_heads, preferred_element_type=jnp.float32)
    d_scores = (probs * (d_probs - delta[..., None])).astype(jnp.bfloat16)
    d_key = (
        jnp.einsum("grqk,qgrd->kgd", d_scores, q_heads, preferred_element_type=jnp.float32)
        * PRE_SCALE
    )
    if want_query:
        d_query = (
            jnp.einsum("grqk,kgd->qgrd", d_scores, k_heads, preferred_element_type=jnp.float32)
            * PRE_SCALE
        )
        d_query = d_query.reshape(n_query, -1)
    else:
        d_query = None
    return (d_query, d_key.reshape(n_key, -1), d_value.reshape(n_key, -1))


def tile_pass(q_part, g_part, k_part, v_part, allowed):
    n_query = q_part.shape[0]
    n_key = k_part.shape[0]
    kv_groups = k_part.shape[1] // HEAD_WIDTH
    scores = scores_of(q_part, k_part, allowed)
    row_max = jnp.max(scores, axis=3, keepdims=True)
    row_total = jnp.sum(jnp.exp(scores - row_max), axis=3, keepdims=True)
    log_total = row_max + jnp.log(row_total)
    probs = jnp.exp(scores - log_total)
    v_heads = v_part.reshape(n_key, kv_groups, HEAD_WIDTH)
    attended = jnp.einsum(
        "grqk,kgd->qgrd", probs.astype(jnp.bfloat16), v_heads, preferred_element_type=jnp.float32
    )
    g_heads = g_part.reshape(n_query, kv_groups, -1, HEAD_WIDTH)
    delta = jnp.transpose(jnp.sum(g_heads.astype(jnp.float32) * attended, axis=3), (1, 2, 0))
    d_query, d_key, d_value = grads_from(probs, q_part, g_part, k_part, v_part, delta, True)
    return (d_query, d_key, d_value, log_total[..., 0], delta)


def on_device(query, key, value, out_grad, block_mask):
    q_seg, k_seg, v_seg, g_seg = (
        lax.all_to_all(query, "head", split_axis=1, concat_axis=0, tiled=True),
        lax.all_to_all(key, "head", split_axis=1, concat_axis=0, tiled=True),
        lax.all_to_all(value, "head", split_axis=1, concat_axis=0, tiled=True),
        lax.all_to_all(out_grad, "head", split_axis=1, concat_axis=0, tiled=True),
    )
    seg_len = q_seg.shape[0]
    tile_rows = BLOCK
    n_tiles = seg_len // tile_rows
    span = tile_rows + WINDOW
    kv_groups = k_seg.shape[1] // HEAD_WIDTH
    per_group = q_seg.shape[1] // k_seg.shape[1]
    seg_anchor = lax.axis_index("ctx") * seg_len
    own_rows = lax.dynamic_slice_in_dim(block_mask, seg_anchor // BLOCK, seg_len // BLOCK, 0)
    k_prev, v_prev = shifted((k_seg[seg_len - WINDOW :], v_seg[seg_len - WINDOW :]), "ctx", 1)
    k_ext = jnp.concatenate([k_prev, k_seg], 0)
    v_ext = jnp.concatenate([v_prev, v_seg], 0)

    def step_fn(state_pair, tile_index):
        d_key_acc, d_value_acc = state_pair
        first_row = tile_index * tile_rows
        q_part = lax.dynamic_slice_in_dim(q_seg, first_row, tile_rows, 0)
        g_part = lax.dynamic_slice_in_dim(g_seg, first_row, tile_rows, 0)
        k_part = lax.dynamic_slice_in_dim(k_ext, first_row, span, 0)
        v_part = lax.dynamic_slice_in_dim(v_ext, first_row, span, 0)
        mask_rows = lax.dynamic_slice_in_dim(own_rows, first_row // BLOCK, tile_rows // BLOCK, 0)
        allowed = allowed_mask(mask_rows, tile_rows, span, WINDOW, seg_anchor + first_row - WINDOW)
        d_query, d_key, d_value, log_total, delta = tile_pass(
            q_part, g_part, k_part, v_part, allowed
        )
        d_key_acc = lax.dynamic_update_slice_in_dim(
            d_key_acc, lax.dynamic_slice_in_dim(d_key_acc, first_row, span, 0) + d_key, first_row, 0
        )
        d_value_acc = lax.dynamic_update_slice_in_dim(
            d_value_acc,
            lax.dynamic_slice_in_dim(d_value_acc, first_row, span, 0) + d_value,
            first_row,
            0,
        )
        return ((d_key_acc, d_value_acc), (d_query.astype(jnp.bfloat16), log_total, delta))

    tile_ids = jnp.arange(n_tiles, dtype=jnp.int32)
    zero_acc = jnp.zeros((seg_len + WINDOW, k_seg.shape[1]), jnp.float32)
    (d_key_ext, d_value_ext), (d_query, lse_tiles, delta_tiles) = lax.scan(
        step_fn, (zero_acc, zero_acc), tile_ids
    )
    query_grad = d_query.reshape(seg_len, -1)
    lse_all = jnp.transpose(lse_tiles, (1, 2, 0, 3)).reshape(kv_groups, per_group, seg_len)
    delta_all = jnp.transpose(delta_tiles, (1, 2, 0, 3)).reshape(kv_groups, per_group, seg_len)
    q_next, g_next = shifted((q_seg[:WINDOW], g_seg[:WINDOW]), "ctx", -1)
    lse_next, delta_next = shifted((lse_all[:, :, :WINDOW], delta_all[:, :, :WINDOW]), "ctx", -1)
    next_rows = lax.dynamic_slice_in_dim(
        block_mask, (seg_anchor + seg_len) // BLOCK, WINDOW // BLOCK, 0
    )
    allowed_next = allowed_mask(next_rows, WINDOW, WINDOW, WINDOW, seg_anchor + seg_len - WINDOW)
    k_last = k_seg[seg_len - WINDOW :]
    v_last = v_seg[seg_len - WINDOW :]
    probs_next = jnp.exp(scores_of(q_next, k_last, allowed_next) - lse_next[..., None])
    _, key_back, value_back = grads_from(
        probs_next, q_next, g_next, k_last, v_last, delta_next, False
    )
    lead_zeros = jnp.zeros((seg_len - WINDOW, k_seg.shape[1]), jnp.float32)
    key_grad = (d_key_ext[WINDOW:] + jnp.concatenate([lead_zeros, key_back], 0)).astype(
        jnp.bfloat16
    )
    value_grad = (d_value_ext[WINDOW:] + jnp.concatenate([lead_zeros, value_back], 0)).astype(
        jnp.bfloat16
    )
    return (
        lax.all_to_all(query_grad, "head", split_axis=0, concat_axis=1, tiled=True),
        lax.all_to_all(key_grad, "head", split_axis=0, concat_axis=1, tiled=True),
        lax.all_to_all(value_grad, "head", split_axis=0, concat_axis=1, tiled=True),
    )


def solution(mesh):
    in_specs = (
        P(("ctx", "head"), None),
        P(("ctx", "head"), None),
        P(("ctx", "head"), None),
        P(("ctx", "head"), None),
        P(),
    )
    out_specs = (P(("ctx", "head"), None), P(("ctx", "head"), None), P(("ctx", "head"), None))
    return jax.shard_map(
        on_device, mesh=mesh, in_specs=in_specs, out_specs=out_specs, check_vma=False
    )
```

profile of v0, /device:TPU:22, one launch (start us, length us, event | category | flops | bytes accessed | tf_op | source)
XLA Modules:
  0.0 698.1 jit_solution(2207444171564713543)
XLA Ops:
  11.0 20.9 %all-to-all-done.1 = bf16[512,4,512]{2,0,1:T(8,128)(2,1)S(1)} async-done(((bf16[512,4,512]{2,0,1:T(8,128)(2,1)}), bf16[512,4,512]{2,0,1:T(8,128)(2,1)S(1)}, u32[]{:S(2)}, u32[]{:S(2)}) %all-to-all-start.1) | async-done | bytes 2097184 | tf_op jit(solution)/shard_map/all_to_all | solution.py:100
  31.9 6.1 all-to-all-start.2
  38.0 6.4 copy.195
  44.4 17.7 %all-to-all-done.2 = bf16[512,4,512]{2,0,1:T(8,128)(2,1)} async-done(((bf16[512,4,512]{2,0,1:T(8,128)(2,1)}), bf16[512,4,512]{2,0,1:T(8,128)(2,1)}, u32[]{:S(2)}, u32[]{:S(2)}) %all-to-all-start.2) | async-done | bytes 2097184 | tf_op jit(solution)/shard_map/all_to_all | solution.py:101
  62.1 6.5 all-to-all-start
  68.6 6.5 copy.204
  75.1 40.1 %all-to-all-done = bf16[512,4,1024]{0,2,1:T(8,128)(2,1)} async-done(((bf16[512,4,1024]{0,2,1:T(8,128)(2,1)}), bf16[512,4,1024]{0,2,1:T(8,128)(2,1)}, u32[]{:S(2)}, u32[]{:S(2)}) %all-to-all-start) | async-done | bytes 4194336 | tf_op jit(solution)/shard_map/all_to_all | solution.py:99
  115.2 6.6 all-to-all-start.3
  155.1 18.0 %collective-permute-done.1 = bf16[1024,512]{0,1:T(8,128)(2,1)} collective-permute-done((bf16[1024,512]{0,1:T(8,128)(2,1)}, bf16[1024,512]{0,1:T(8,128)(2,1)}, u32[]{:S(2)}, u32[]{:S(2)}) %collective-permute-start.1) | collective-permute-done | bytes 1048608 | tf_op jit(solution)/shard_map/ppermute | solution.py:17
  176.2 6.3 copy.196
  190.2 6.3 copy.205
  210.1 352.3 %while.20 = (s32[]{:T(128)}, f32[3072,512]{0,1:T(8,128)}, f32[3072,512]{0,1:T(8,128)}, bf16[16,128,1024]{2,1,0:T(8,128)(2,1)}, f32[16,4,2,128]{3,2,1,0:T(2,128)S...) while((s32[]{:T(128)}, f32[3072,512]{0,1:T(8,128)}, ...), condition=%wide.region_5.6_spmd, body=%wide.region_0.5_spmd.sunk | while | flops 1830584960 | bytes 64059684 | solution.py:141
  226.4 5.8 constant_dynamic-update-slice_fusion.5
  248.5 5.8 constant_dynamic-update-slice_fusion.5
  336.6 5.8 constant_dynamic-update-slice_fusion.5
  468.7 5.8 constant_dynamic-update-slice_fusion.5
  573.9 14.8 %fusion.39 = f32[4,1024,1024,2]{2,1,3,0:T(8,128)} fusion(bf16[1024,4,2,128]{0,3,2,1:T(8,128)(2,1)} %bitcast.48, bf16[1024,4,128,1]{2,1,0,3:T(4,128)(2,1)S(1)} %bitcast.245), kind=kOutput, calls=%fused_computation.69 | convolution fusion | flops 2147483648 | bytes 36700160 | tf_op jit(solution)/shard_map/qgrd,kgd->grqk/dot_general | solution.py:44
  588.6 16.6 %fusion.22 = f32[4,1024,128,1]{1,2,3,0:T(8,128)} fusion(bf16[1024,4,2,128]{0,3,2,1:T(8,128)(2,1)} %bitcast.53, f32[4,1024,1024,2]{2,1,3,0:T(8,128)} %fusion.39, f32[4,2,1024]{2,1,0:T(2,128)S(1)} %collective-permute-done.3, pred[1024,1024]{0,1:T(8,128)(4,1)S(1)} %copy-done.3), kind=kOutput, calls=%fused_computation.50 | convolution fusion | flops 2181038080 | bytes 38830080 | tf_op jit(solution)/shard_map/grqk,qgrd->kgd/dot_general | solution.py:58
  605.2 20.8 %bitcast_multiply_fusion = f32[4,1024,128]{1,2,0:T(8,128)} fusion(bf16[1024,4,2,128]{0,3,2,1:T(8,128)(2,1)} %bitcast.48, f32[4,1024,1024,2]{2,1,3,0:T(8,128)} %fusion.39, f32[4,2,1024]{2,1,0:T(2,128)S(1)} %collective-permute-done.5, f32[4,2,1024]{2,1,0:T(2,128)S(1)} %collective-permute-done.3, pred[1024,1024]{0,1:T(8,128)(4,1)S(1)} %copy-done.3, ...), kind=kOutput, calls=%fused_computation.67 | convolution fusion | flops 4345823232 | bytes 42008576 | tf_op jit(solution)/shard_map/grqk,qgrd->kgd/dot_general | solution.py:64
  626.0 6.5 add_convert_fusion
  642.6 20.1 %all-to-all-done.6 = bf16[4,512,512]{2,1,0:T(8,128)(2,1)S(1)} async-done(((bf16[4,512,512]{2,1,0:T(8,128)(2,1)}), bf16[4,512,512]{2,1,0:T(8,128)(2,1)S(1)}, u32[]{:S(2)}, u32[]{:S(2)}) %all-to-all-start.6) | async-done | bytes 2097184 | tf_op jit(solution)/shard_map/all_to_all | solution.py:169
  662.7 6.1 all-to-all-start.5
  668.8 6.2 copy.209
  675.0 6.3 copy.225
  (497 shorter events, 422.8 us)
Async XLA Ops:
  0.6 126.1 %copy-start = (s32[128,9]{0,1:T(8,128)S(1)}, s32[128,9]{0,1:T(8,128)}, u32[]{:S(2)}) copy-start(s32[128,9]{0,1:T(8,128)} %param.11) | copy-start | bytes 13828
  3.8 28.1 %all-to-all-start.1 = ((bf16[512,4,512]{2,0,1:T(8,128)(2,1)}), bf16[512,4,512]{2,0,1:T(8,128)(2,1)S(1)}, u32[]{:S(2)}, u32[]{:S(2)}) async-start(bf16[512,4,512]{2,0,1:T(8,128)(2,1)} %bitcast.240), calls=%async_computation.1 | async-start | bytes 4194304 | tf_op jit(solution)/shard_map/all_to_all | solution.py:100
  31.9 30.2 %all-to-all-start.2 = ((bf16[512,4,512]{2,0,1:T(8,128)(2,1)}), bf16[512,4,512]{2,0,1:T(8,128)(2,1)}, u32[]{:S(2)}, u32[]{:S(2)}) async-start(bf16[512,4,512]{2,0,1:T(8,128)(2,1)} %bitcast.239), calls=%async_computation.2 | async-start | bytes 4194304 | tf_op jit(solution)/shard_map/all_to_all | solution.py:101
  62.1 53.2 %all-to-all-start = ((bf16[512,4,1024]{0,2,1:T(8,128)(2,1)}), bf16[512,4,1024]{0,2,1:T(8,128)(2,1)}, u32[]{:S(2)}, u32[]{:S(2)}) async-start(bf16[512,4,1024]{0,2,1:T(8,128)(2,1)} %bitcast.227), calls=%async_computation | async-start | bytes 8388608 | tf_op jit(solution)/shard_map/all_to_all | solution.py:99
  115.2 74.9 %all-to-all-start.3 = ((bf16[512,4,1024]{0,2,1:T(8,128)(2,1)}), bf16[512,4,1024]{0,2,1:T(8,128)(2,1)}, u32[]{:S(2)}, u32[]{:S(2)}) async-start(bf16[512,4,1024]{0,2,1:T(8,128)(2,1)} %bitcast.226), calls=%async_computation.3 | async-start | bytes 8388608 | tf_op jit(solution)/shard_map/all_to_all | solution.py:102
  123.2 28.2 %collective-permute-start = (bf16[1024,512]{0,1:T(8,128)(2,1)}, bf16[1024,512]{0,1:T(8,128)(2,1)}, u32[]{:S(2)}, u32[]{:S(2)}) collective-permute-start(bf16[1024,512]{0,1:T(8,128)(2,1)} %copy.252), channel_id=1, source_target_pairs={{0,4},{4,8},{8,12},{12,16},{16,20},{20,24},{24,28},{1,5},{5,9},{9,... | collective-permute-start | bytes 3145736 | tf_op jit(solution)/shard_map/ppermute | solution.py:17
  131.6 41.5 %collective-permute-start.1 = (bf16[1024,512]{0,1:T(8,128)(2,1)}, bf16[1024,512]{0,1:T(8,128)(2,1)}, u32[]{:S(2)}, u32[]{:S(2)}) collective-permute-start(bf16[1024,512]{0,1:T(8,128)(2,1)} %copy.254), channel_id=1, source_target_pairs={{0,4},{4,8},{8,12},{12,16},{16,20},{20,24},{24,28},{1,5},{5,9},{9,... | collective-permute-start | bytes 3145736 | tf_op jit(solution)/shard_map/ppermute | solution.py:17
  186.8 387.0 %collective-permute-start.2 = (bf16[1024,1024]{0,1:T(8,128)(2,1)}, bf16[1024,1024]{0,1:T(8,128)(2,1)}, u32[]{:S(2)}, u32[]{:S(2)}) collective-permute-start(bf16[1024,1024]{0,1:T(8,128)(2,1)} %copy.211), channel_id=1, source_target_pairs={{4,0},{8,4},{12,8},{16,12},{20,16},{24,20},{28,24},{5,1},{9,5},{13... | collective-permute-start | bytes 6291464 | tf_op jit(solution)/shard_map/ppermute | solution.py:17
  200.9 387.8 %collective-permute-start.4 = (bf16[1024,1024]{0,1:T(8,128)(2,1)}, bf16[1024,1024]{0,1:T(8,128)(2,1)}, u32[]{:S(2)}, u32[]{:S(2)}) collective-permute-start(bf16[1024,1024]{0,1:T(8,128)(2,1)} %copy.215), channel_id=1, source_target_pairs={{4,0},{8,4},{12,8},{16,12},{20,16},{24,20},{28,24},{5,1},{9,5},{13... | collective-permute-start | bytes 6291464 | tf_op jit(solution)/shard_map/ppermute | solution.py:17
  562.5 11.4 %copy-start.2 = (bf16[1024,4,128]{2,1,0:T(4,128)(2,1)S(1)}, bf16[1024,4,128]{2,1,0:T(4,128)(2,1)}, u32[]{:S(2)}) copy-start(bf16[1024,4,128]{2,1,0:T(4,128)(2,1)} %reshape.234) | copy-start | bytes 3145732
  562.5 72.5 %all-to-all-start.4 = ((bf16[4,512,1024]{2,1,0:T(8,128)(2,1)}), bf16[4,512,1024]{2,1,0:T(8,128)(2,1)}, u32[]{:S(2)}, u32[]{:S(2)}) async-start(bf16[4,512,1024]{2,1,0:T(8,128)(2,1)} %bitcast.246), calls=%async_computation.4 | async-start | bytes 8388608 | tf_op jit(solution)/shard_map/all_to_all | solution.py:167
  567.8 37.4 %collective-permute-start.5 = (f32[4,2,1024]{2,1,0:T(2,128)S(1)}, f32[4,2,1024]{2,1,0:T(2,128)S(1)}, u32[]{:S(2)}, u32[]{:S(2)}) collective-permute-start(f32[4,2,1024]{2,1,0:T(2,128)S(1)} %slice.55), channel_id=1, source_target_pairs={{4,0},{8,4},{12,8},{16,12},{20,16},{24,20},{28,24},{5,1},{9,5},{13... | collective-permute-start | bytes 98312 | tf_op jit(solution)/shard_map/ppermute | solution.py:17
  571.2 17.4 %collective-permute-start.3 = (f32[4,2,1024]{2,1,0:T(2,128)S(1)}, f32[4,2,1024]{2,1,0:T(2,128)S(1)}, u32[]{:S(2)}, u32[]{:S(2)}) collective-permute-start(f32[4,2,1024]{2,1,0:T(2,128)S(1)} %slice.53), channel_id=1, source_target_pairs={{4,0},{8,4},{12,8},{16,12},{20,16},{24,20},{28,24},{5,1},{9,5},{13... | collective-permute-start | bytes 98312 | tf_op jit(solution)/shard_map/ppermute | solution.py:17
  573.9 14.8 %copy-start.3 = (pred[1024,1024]{0,1:T(8,128)(4,1)S(1)}, pred[1024,1024]{0,1:T(8,128)(4,1)}, u32[]{:S(2)}) copy-start(pred[1024,1024]{0,1:T(8,128)(4,1)} %fusion.34) | copy-start | bytes 3145732
  588.6 16.6 %copy-start.4 = (bf16[1024,4,128]{2,1,0:T(4,128)(2,1)S(1)}, bf16[1024,4,128]{2,1,0:T(4,128)(2,1)}, u32[]{:S(2)}) copy-start(bf16[1024,4,128]{2,1,0:T(4,128)(2,1)} %reshape.237) | copy-start | bytes 3145732
  635.0 27.7 %all-to-all-start.6 = ((bf16[4,512,512]{2,1,0:T(8,128)(2,1)}), bf16[4,512,512]{2,1,0:T(8,128)(2,1)S(1)}, u32[]{:S(2)}, u32[]{:S(2)}) async-start(bf16[4,512,512]{2,1,0:T(8,128)(2,1)} %bitcast.238), calls=%async_computation.6 | async-start | bytes 4194304 | tf_op jit(solution)/shard_map/all_to_all | solution.py:169
  662.7 30.2 %all-to-all-start.5 = ((bf16[4,512,512]{2,1,0:T(8,128)(2,1)}), bf16[4,512,512]{2,1,0:T(8,128)(2,1)}, u32[]{:S(2)}, u32[]{:S(2)}) async-start(bf16[4,512,512]{2,1,0:T(8,128)(2,1)} %bitcast.237), calls=%async_computation.5 | async-start | bytes 4194304 | tf_op jit(solution)/shard_map/all_to_all | solution.py:168
  683.7 14.4 %copy-start.1 = (s32[128,9]{0,1:T(8,128)S(1)}, s32[128,9]{0,1:T(8,128)}, u32[]{:S(2)}) copy-start(s32[128,9]{0,1:T(8,128)} %param.11) | copy-start | bytes 13828
where the time goes:
time: 705 us; the launch traced here: 698 us
  local copies, waits for them, and re-layouts  198 us (28%)
  matrix products  165 us (23%)
  other arithmetic  138 us (20%)
  waiting for transfers between devices  127 us (18%)
  starting transfers between devices  57 us (8%)
  loops' own time  12.3 us (2%)
    dynamic_update_slice x16, other arithmetic, step_fn(): lax.dynamic_update_slice_in_dim(d_value_acc, lax.dynamic_slice_in_dim(d_v...  92.2 us
    dot_general x17, matrix products, grads_from(): jnp.einsum('grqk,qgrd->kgd', probs.astype(jnp.bfloat16), g_heads, preferr...  54 us
    all_to_all x1, waiting for transfers between devices, on_device(): lax.all_to_all(query, 'head', split_axis=1, concat_axis=0, tiled=True)  40.1 us
    dot_general x17, matrix products, grads_from(): jnp.einsum('grqk,qgrd->kgd', d_scores, q_heads, preferred_element_type=jn...  34.1 us
    dot_general x17, matrix products, scores_of(): jnp.einsum('qgrd,kgd->grqk', q_heads, k_heads, preferred_element_type=jnp...  30.1 us
    unnamed x16, local copies, waits for them, and re-layouts  25.6 us
    ppermute x6, waiting for transfers between devices, shifted(): return lax.ppermute(block, axis, route)  23.1 us
    dynamic_slice x16, local copies, waits for them, and re-layouts, step_fn(): k_part = lax.dynamic_slice_in_dim(k_ext, first_row, span, 0)  21.9 us
  transfers between devices with their start and end apart: 13, of which 7 were waited for; matrix products, arithmetic and copies ran while one was open for 71% of the time, Pallas kernels for 0%

commit v1 on v0

v1 whole, which is shorter than its diff:
```python
import functools
import math

import jax
import jax.numpy as jnp
from jax import lax
from jax.experimental import pallas as pl
from jax.experimental.pallas import tpu as pltpu
from jax.sharding import PartitionSpec as P

HEAD_WIDTH = 128
WINDOW = 1024
BLOCK = 128
PRE_SCALE = 168.0 ** (-0.5)
LOG2_SCALE = PRE_SCALE * math.log2(math.e)
AXES = ("ctx", "head")
CHUNKS = 4
NT = (((1,), (1,)), ((), ()))
NN = (((1,), (0,)), ((), ()))


def moved(block, distance):
    n = lax.axis_size(AXES[0]) * lax.axis_size(AXES[1])
    route = [(i, i + distance) for i in range(n) if 0 <= i + distance < n]
    return lax.ppermute(block, AXES, route)


def swapped(block):
    n = lax.axis_size(AXES[0]) * lax.axis_size(AXES[1])
    return lax.ppermute(block, AXES, [(i, i ^ 1) for i in range(n)])


def pack_kernel(k_ref, v_ref, out_ref):
    out_ref[:, :HEAD_WIDTH] = k_ref[...]
    out_ref[:, HEAD_WIDTH:] = v_ref[...]


def packed(key, value, first, heads):
    rows = key.shape[0]
    spec = pl.BlockSpec((rows, HEAD_WIDTH), lambda h: (0, first + h))
    return pl.pallas_call(
        pack_kernel,
        out_shape=jax.ShapeDtypeStruct((rows, heads * 2 * HEAD_WIDTH), key.dtype),
        grid=(heads,),
        in_specs=[spec, spec],
        out_specs=pl.BlockSpec((rows, 2 * HEAD_WIDTH), lambda h: (0, h)),
        name="pack_key_value",
    )(key, value)


def dot(a, b, dims):
    return lax.dot_general(a, b, dims, preferred_element_type=jnp.float32)


def attention_kernel(n_pieces, per_group, chained, *refs):
    bias_ref, q_ref, g_ref, k_ref, v_ref = refs[:5]
    piece_refs = refs[5 : 5 + n_pieces]
    rest = refs[5 + n_pieces + (1 if chained else 0) :]
    dq_ref, down_ref = rest[:2]
    dpiece_refs = rest[2 : 2 + n_pieces]
    k_ext, v_ext, k_turned, q_all, g_all, p_all, ds_all = rest[2 + n_pieces :]
    rows = q_ref.shape[0]
    tiles = rows // BLOCK
    lead = n_pieces * rows
    wide = per_group * BLOCK
    span = WINDOW + BLOCK
    n_off = span // BLOCK
    w = HEAD_WIDTH

    for i, piece in enumerate(piece_refs):
        k_ext[i * rows : (i + 1) * rows, :] = piece[:, :w]
        v_ext[i * rows : (i + 1) * rows, :] = piece[:, w:]
    k_ext[lead:, :] = k_ref[...]
    v_ext[lead:, :] = v_ref[...]
    k_turned[...] = k_ext[...].T
    for b in range(tiles):
        for r in range(per_group):
            at = b * wide + r * BLOCK
            q_all[at : at + BLOCK, :] = q_ref[b * BLOCK : (b + 1) * BLOCK, r * w : (r + 1) * w]
            g_all[at : at + BLOCK, :] = g_ref[b * BLOCK : (b + 1) * BLOCK, r * w : (r + 1) * w]

    k_index = lax.broadcasted_iota(jnp.int32, (BLOCK, wide), 0)
    q_index = lax.rem(lax.broadcasted_iota(jnp.int32, (BLOCK, wide), 1), BLOCK)
    lower = k_index <= q_index

    for b in range(tiles):
        top = b * BLOCK
        cols = slice(b * wide, (b + 1) * wide)
        q_two = q_all[cols, :]
        g_two = g_all[cols, :]
        scores = dot(k_ext[top : top + span, :], q_two, NT)
        parts = [scores[i * BLOCK : (i + 1) * BLOCK] for i in range(n_off)]
        bias = [bias_ref[b, n_off - 1 - i] for i in range(n_off)]
        edge = jnp.where(lower, parts[-1], parts[0] + bias[0])
        inner = parts[1:-1]
        top_score = jnp.max(edge, axis=0, keepdims=True)
        for part, shift in zip(inner, bias[1:-1]):
            top_score = jnp.maximum(top_score, jnp.max(part, axis=0, keepdims=True) + shift)
        top_scaled = top_score * LOG2_SCALE
        weights = [jnp.exp2(edge * LOG2_SCALE - top_scaled)]
        for part, shift in zip(inner, bias[1:-1]):
            weights.append(jnp.exp2(part * LOG2_SCALE - (top_scaled - shift)))
        d_probs = dot(v_ext[top : top + span, :], g_two, NT)
        d_parts = [d_probs[i * BLOCK : (i + 1) * BLOCK] for i in range(n_off)]
        d_parts = [jnp.where(lower, d_parts[-1], d_parts[0])] + d_parts[1:-1]
        total = sum(jnp.sum(x, axis=0, keepdims=True) for x in weights)
        moment = sum(jnp.sum(x * y, axis=0, keepdims=True) for x, y in zip(weights, d_parts))
        inverse = 1.0 / total
        delta = moment * inverse
        for i, (x, y) in enumerate(zip(weights, d_parts)):
            prob = x * inverse
            d_score = prob * (y - delta)
            if i == 0:
                last = slice(top + span - BLOCK, top + span)
                first = slice(top, top + BLOCK)
                p_all[first, cols] = jnp.where(lower, 0.0, prob).astype(jnp.bfloat16)
                p_all[last, cols] = jnp.where(lower, prob, 0.0).astype(jnp.bfloat16)
                ds_all[first, cols] = jnp.where(lower, 0.0, d_score).astype(jnp.bfloat16)
                ds_all[last, cols] = jnp.where(lower, d_score, 0.0).astype(jnp.bfloat16)
            else:
                here = slice(top + i * BLOCK, top + (i + 1) * BLOCK)
                p_all[here, cols] = prob.astype(jnp.bfloat16)
                ds_all[here, cols] = d_score.astype(jnp.bfloat16)
        dq_turned = dot(k_turned[:, top : top + span], ds_all[top : top + span, cols], NN)
        dq_two = dq_turned.T * PRE_SCALE
        for r in range(per_group):
            dq_ref[top : top + BLOCK, r * w : (r + 1) * w] = dq_two[
                r * BLOCK : (r + 1) * BLOCK
            ].astype(dq_ref.dtype)

    n_key = (lead + rows) // BLOCK
    j = 0
    while j < n_key:
        low, high = max(0, j - n_off + 1), min(tiles - 1, j)
        end = j + 1
        while (
            end < n_key
            and (max(0, end - n_off + 1), min(tiles - 1, end)) == (low, high)
            and (end * BLOCK) % rows
        ):
            end += 1
        here = slice(j * BLOCK, end * BLOCK)
        cols = slice(low * wide, (high + 1) * wide)
        dv = dot(p_all[here, cols], g_all[cols, :], NN)
        dk = dot(ds_all[here, cols], q_all[cols, :], NN) * PRE_SCALE
        target = down_ref if j * BLOCK >= lead else dpiece_refs[j * BLOCK // rows]
        at = j * BLOCK % rows
        there = slice(at, at + (end - j) * BLOCK)
        target[there, :w] = dk.astype(target.dtype)
        target[there, w:] = dv.astype(target.dtype)
        j = end


def attention(bias, query, out_grad, key, value, pieces, first, heads, dq_before):
    rows = query.shape[0]
    per_group = query.shape[1] // key.shape[1]
    n = len(pieces)
    w = HEAD_WIDTH
    chained = dq_before is not None
    q_spec = pl.BlockSpec((rows, per_group * w), lambda h: (0, first + h))
    k_spec = pl.BlockSpec((rows, w), lambda h: (0, first + h))
    kv_spec = pl.BlockSpec((rows, 2 * w), lambda h: (0, h))
    in_specs = [pl.BlockSpec(memory_space=pltpu.SMEM), q_spec, q_spec, k_spec, k_spec] + [kv_spec] * n
    operands = [bias, query, out_grad, key, value, *pieces]
    aliases = {}
    if chained:
        aliases = {len(operands): 0}
        in_specs.append(pl.BlockSpec(memory_space=pl.ANY))
        operands.append(dq_before)
    kv_shape = (rows, heads * 2 * w)
    length = (n + 1) * rows
    wide = rows * per_group
    work = heads * wide * (WINDOW + BLOCK)
    bf16 = jnp.bfloat16
    return pl.pallas_call(
        functools.partial(attention_kernel, n, per_group, chained),
        out_shape=[
            jax.ShapeDtypeStruct(query.shape, query.dtype),
            jax.ShapeDtypeStruct(kv_shape, jnp.float32),
        ]
        + [jax.ShapeDtypeStruct(kv_shape, bf16)] * n,
        grid=(heads,),
        in_specs=in_specs,
        out_specs=[q_spec] + [kv_spec] * (n + 1),
        scratch_shapes=[
            pltpu.VMEM((length, w), bf16),
            pltpu.VMEM((length, w), bf16),
            pltpu.VMEM((w, length), bf16),
            pltpu.VMEM((wide, w), bf16),
            pltpu.VMEM((wide, w), bf16),
            pltpu.VMEM((length, wide), bf16),
            pltpu.VMEM((length, wide), bf16),
        ],
        input_output_aliases=aliases,
        compiler_params=pltpu.CompilerParams(vmem_limit_bytes=56 * 1024 * 1024),
        cost_estimate=pl.CostEstimate(
            flops=20 * work * w, bytes_accessed=heads * rows * w * 40, transcendentals=work
        ),
        name="attention_grads",
    )(*operands)


def finish_kernel(n, keep_refs, own_ref, *refs):
    dk_ref, dv_ref = refs[-2:]
    total = own_ref[...]
    for keep, ref in zip(keep_refs, refs[:n]):
        total = total + ref[...].astype(jnp.float32)
    w = HEAD_WIDTH
    dk_ref[...] = total[:, :w].astype(dk_ref.dtype)
    dv_ref[...] = total[:, w:].astype(dv_ref.dtype)


def finished(own, terms, first, heads, shape, before):
    rows = own.shape[0]
    w = HEAD_WIDTH
    kv_spec = pl.BlockSpec((rows, 2 * w), lambda h: (0, h))
    out_spec = pl.BlockSpec((rows, w), lambda h: (0, first + h))
    operands = [own, *terms]
    in_specs = [kv_spec] * len(operands)
    aliases = {}
    if before is not None:
        aliases = {len(operands): 0, len(operands) + 1: 1}
        operands += list(before)
        in_specs += [pl.BlockSpec(memory_space=pl.ANY)] * 2
    return pl.pallas_call(
        functools.partial(finish_kernel, len(terms), [True] * len(terms)),
        out_shape=[jax.ShapeDtypeStruct(shape, jnp.bfloat16)] * 2,
        grid=(heads,),
        in_specs=in_specs,
        out_specs=[out_spec] * 2,
        input_output_aliases=aliases,
        name="sum_key_value_grads",
    )(*operands)


def on_device(query, key, value, out_grad, block_mask):
    rows = query.shape[0]
    kv_heads = key.shape[1] // HEAD_WIDTH
    n_pieces = WINDOW // rows
    n_head = lax.axis_size("head")
    device = lax.axis_index("ctx") * n_head + lax.axis_index("head")
    first_block = device * (rows // BLOCK)
    own_rows = lax.dynamic_slice_in_dim(block_mask, first_block, rows // BLOCK, 0)
    block = first_block + lax.broadcasted_iota(jnp.int32, own_rows.shape, 0)
    offset = lax.broadcasted_iota(jnp.int32, own_rows.shape, 1)
    usable = (own_rows > 0) & (block >= offset)
    bias = jnp.where(usable, 0.0, -jnp.inf).astype(jnp.float32)
    paired = n_pieces == 2 and n_head % 2 == 0
    odd = lax.rem(device, 2) == 1

    n_chunks = CHUNKS if kv_heads % CHUNKS == 0 else 1
    heads = kv_heads // n_chunks
    bf16 = jnp.bfloat16
    f32 = jnp.float32

    packs = [packed(key, value, i * heads, heads) for i in range(n_chunks)]
    if paired:
        far = [moved(x, 2) for x in packs]
        near = [swapped(jnp.where(odd, x, y)) for x, y in zip(far, packs)]
        pieces = [[x, y] for x, y in zip(far, near)]
    else:
        pieces = [[moved(x, j) for j in range(n_pieces, 0, -1)] for x in packs]

    dq = None
    grads = None
    for i in range(n_chunks):
        out = attention(bias, query, out_grad, key, value, pieces[i], i * heads, heads, dq)
        dq, own = out[:2]
        if paired:
            d_far, d_near = out[2:]
            from_pair = swapped(d_near)
            for_far = jnp.where(odd, d_far.astype(f32) + from_pair.astype(f32), d_far.astype(f32))
            back = moved(for_far.astype(bf16), -2)
            pair_term = jnp.where(odd, jnp.zeros_like(from_pair), from_pair)
            terms = [back, pair_term]
        else:
            terms = [moved(x, j - n_pieces) for j, x in enumerate(out[2:])]
        grads = finished(own, terms, i * heads, heads, key.shape, grads)
    return (dq, grads[0], grads[1])


def solution(mesh):
    split = P(("ctx", "head"), None)
    return jax.shard_map(
        on_device,
        mesh=mesh,
        in_specs=(split, split, split, split, P()),
        out_specs=(split, split, split),
        check_vma=False,
    )
```

time: 705 us -> 293 us (0.42)
  local copies, waits for them, and re-layouts: 198 us -> 4.23 us
  matrix products: 165 us -> 0 us
  other arithmetic: 138 us -> 7.16 us
  Pallas kernels: 0 us -> 118 us
  starting transfers between devices: 57 us -> 28.1 us
  loops' own time: 12.3 us -> 0 us
    dot_general x99 -> x0, matrix products: 165 us -> none  [the longest x17 54 us: grads_from(): jnp.einsum('grqk,qgrd->kgd', probs.astype(jnp.bfloat16), g_heads, preferr...]
    pallas_call x0 -> x12, Pallas kernels: none -> 118 us  [the longest x4 87.9 us: attention(): pl.pallas_call(functools.partial(attention_kernel, n, per_group, chained)...]
    ppermute x6 -> x16, waiting for transfers between devices: 23.1 us -> 134 us  [the longest x8 134 us: moved(): return lax.ppermute(block, AXES, route)]
    all_to_all x7 -> x0, waiting for transfers between devices: 104 us -> none  [the longest x1 40.1 us: on_device(): lax.all_to_all(query, 'head', split_axis=1, concat_axis=0, tiled=True)]
    dynamic_update_slice x32 -> x0, other arithmetic: 92.5 us -> none  [the longest x16 92.2 us: step_fn(): lax.dynamic_update_slice_in_dim(d_value_acc, lax.dynamic_slice_in_dim(d_v...]
    dynamic_slice x115 -> x1, local copies, waits for them, and re-layouts: 90.1 us -> 0.07 us  [on_device(): lax.dynamic_slice_in_dim(block_mask, first_block, rows // BLOCK, 0)]
    all_to_all x7 -> x0, starting transfers between devices: 38.3 us -> none  [the longest x1 6.56 us: on_device(): lax.all_to_all(out_grad, 'head', split_axis=1, concat_axis=0, tiled=True)]
    all_to_all x9 -> x0, local copies, waits for them, and re-layouts: 35.5 us -> none  [the longest x1 6.33 us: on_device(): lax.all_to_all(out_grad, 'head', split_axis=1, concat_axis=0, tiled=True)]
  transfers between devices with their start and end apart: 13 -> 16, of which waited for: 7 -> 8; matrix products, arithmetic and copies ran while one was open for 71% -> 3% of each run, Pallas kernels for 0% -> 38%
where the time goes in v1:
time: 293 us; the launch traced here: 292 us
  waiting for transfers between devices  134 us (46%)
  Pallas kernels  118 us (40%)
  starting transfers between devices  28.1 us (10%)
  other arithmetic  7.16 us (2%)
  local copies, waits for them, and re-layouts  4.23 us (1%)
    ppermute x8, waiting for transfers between devices, moved(): return lax.ppermute(block, AXES, route)  134 us
    pallas_call x4, Pallas kernels, attention(): pl.pallas_call(functools.partial(attention_kernel, n, per_group, chained)...  87.9 us
    ppermute x8, starting transfers between devices, moved(): return lax.ppermute(block, AXES, route)  26.6 us
    pallas_call x4, Pallas kernels, finished(): pl.pallas_call(functools.partial(finish_kernel, len(terms), [True] * len(...  15.9 us
    pallas_call x4, Pallas kernels, packed(): pl.pallas_call(pack_kernel, out_shape=jax.ShapeDtypeStruct((rows, heads *...  14 us
  transfers between devices with their start and end apart: 16, of which 8 were waited for; matrix products, arithmetic and copies ran while one was open for 3% of the time, Pallas kernels for 38%

profile of v1, /device:TPU:22, one launch (start us, length us, event | category | flops | bytes accessed | tf_op | source)
XLA Modules:
  0.0 292.2 jit_solution(15520674034961812080)
XLA Ops:
  0.6 3.5 %pack_key_value.7 = bf16[512,1024]{1,0:T(8,128)(2,1)} custom-call(bf16[512,2048]{1,0:T(8,128)(2,1)} %refs_3_.7, bf16[512,2048]{1,0:T(8,128)(2,1)} %refs_4_.7), custom_call_target="tpu_custom_call" | custom-call | tf_op jit(solution)/shard_map/pack_key_value/pallas_call | solution.py:41
  7.6 3.5 %pack_key_value.6 = bf16[512,1024]{1,0:T(8,128)(2,1)} custom-call(bf16[512,2048]{1,0:T(8,128)(2,1)} %refs_3_.7, bf16[512,2048]{1,0:T(8,128)(2,1)} %refs_4_.7), custom_call_target="tpu_custom_call" | custom-call | tf_op jit(solution)/shard_map/pack_key_value/pallas_call | solution.py:41
  14.5 3.5 %pack_key_value.5 = bf16[512,1024]{1,0:T(8,128)(2,1)} custom-call(bf16[512,2048]{1,0:T(8,128)(2,1)} %refs_3_.7, bf16[512,2048]{1,0:T(8,128)(2,1)} %refs_4_.7), custom_call_target="tpu_custom_call" | custom-call | tf_op jit(solution)/shard_map/pack_key_value/pallas_call | solution.py:41
  18.0 3.5 %collective-permute-start.2 = (bf16[512,1024]{1,0:T(8,128)(2,1)}, bf16[512,1024]{1,0:T(8,128)(2,1)}, u32[]{:S(2)}, u32[]{:S(2)}) collective-permute-start(bf16[512,1024]{1,0:T(8,128)(2,1)} %pack_key_value.5), channel_id=1, source_target_pairs={{0,2},{1,3},{2,4},{3,5},{4,6},{5,7},{6,8},{7,9},{8,10},{9,11},{10,... | collective-permute-start | bytes 3145736 | tf_op jit(solution)/shard_map/ppermute | solution.py:25
  21.4 3.5 %pack_key_value.4 = bf16[512,1024]{1,0:T(8,128)(2,1)} custom-call(bf16[512,2048]{1,0:T(8,128)(2,1)} %refs_3_.7, bf16[512,2048]{1,0:T(8,128)(2,1)} %refs_4_.7), custom_call_target="tpu_custom_call" | custom-call | tf_op jit(solution)/shard_map/pack_key_value/pallas_call | solution.py:41
  24.9 3.5 %collective-permute-start = (bf16[512,1024]{1,0:T(8,128)(2,1)}, bf16[512,1024]{1,0:T(8,128)(2,1)S(1)}, u32[]{:S(2)}, u32[]{:S(2)}) collective-permute-start(bf16[512,1024]{1,0:T(8,128)(2,1)} %pack_key_value.4), channel_id=1, source_target_pairs={{0,2},{1,3},{2,4},{3,5},{4,6},{5,7},{6,8},{7,9},{8,10},{9,11},{10,... | collective-permute-start | bytes 3145736 | tf_op jit(solution)/shard_map/ppermute | solution.py:25
  28.7 3.7 %collective-permute-done.6.refs_5_ = bf16[512,1024]{1,0:T(8,128)(2,1)} collective-permute-done((bf16[512,1024]{1,0:T(8,128)(2,1)}, bf16[512,1024]{1,0:T(8,128)(2,1)}, u32[]{:S(2)}, u32[]{:S(2)}) %collective-permute-start.6) | collective-permute-done | bytes 1048608 | tf_op jit(solution)/shard_map/ppermute | solution.py:25
  33.3 21.6 %collective-permute-done.4.refs_5_ = bf16[512,1024]{1,0:T(8,128)(2,1)} collective-permute-done((bf16[512,1024]{1,0:T(8,128)(2,1)}, bf16[512,1024]{1,0:T(8,128)(2,1)}, u32[]{:S(2)}, u32[]{:S(2)}) %collective-permute-start.4) | collective-permute-done | bytes 1048608 | tf_op jit(solution)/shard_map/ppermute | solution.py:25
  55.2 22.2 %collective-permute-done.2.refs_5_ = bf16[512,1024]{1,0:T(8,128)(2,1)} collective-permute-done((bf16[512,1024]{1,0:T(8,128)(2,1)}, bf16[512,1024]{1,0:T(8,128)(2,1)}, u32[]{:S(2)}, u32[]{:S(2)}) %collective-permute-start.2) | collective-permute-done | bytes 1048608 | tf_op jit(solution)/shard_map/ppermute | solution.py:25
  77.6 21.0 %collective-permute-done.refs_5_ = bf16[512,1024]{1,0:T(8,128)(2,1)S(1)} collective-permute-done((bf16[512,1024]{1,0:T(8,128)(2,1)}, bf16[512,1024]{1,0:T(8,128)(2,1)S(1)}, u32[]{:S(2)}, u32[]{:S(2)}) %collective-permute-start) | collective-permute-done | bytes 1048608 | tf_op jit(solution)/shard_map/ppermute | solution.py:25
  99.9 21.9 %attention_grads.4 = (bf16[512,4096]{1,0:T(8,128)(2,1)}, f32[512,1024]{1,0:T(8,128)}, bf16[512,1024]{1,0:T(8,128)(2,1)}, bf16[512,1024]{1,0:T(8,128)(2,1)}) custom-call(f32[4,9]{1,0:T(4,128)} %fusion.5.refs_0_, bf16[512,4096]{1,0:T(8,128)(2,1)} %refs_1_.7, bf16[512,4096]{1,0:T(8,128)(2,1)} %refs_2_.7, bf16[512,2048]{1,0:T(8,128)(2,1)} %refs_3_.7, ...), custom_call_target="tpu_custom_call" | custom-call | flops 12079595520 | bytes 10485760 | tf_op jit(solution)/shard_map/attention_grads/pallas_call | solution.py:175
  122.2 21.9 %attention_grads.5 = (bf16[512,4096]{1,0:T(8,128)(2,1)}, f32[512,1024]{1,0:T(8,128)}, bf16[512,1024]{1,0:T(8,128)(2,1)}, bf16[512,1024]{1,0:T(8,128)(2,1)}) custom-call(f32[4,9]{1,0:T(4,128)} %fusion.5.refs_0_, bf16[512,4096]{1,0:T(8,128)(2,1)} %refs_1_.7, bf16[512,4096]{1,0:T(8,128)(2,1)} %refs_2_.7, ...), custom_call_target="tpu_custom_call", output_to_operand_aliasing={{0}: (7, {})} | custom-call | flops 12079595520 | bytes 10485760 | tf_op jit(solution)/shard_map/attention_grads/pallas_call | solution.py:175
  145.3 22.1 %attention_grads.6 = (bf16[512,4096]{1,0:T(8,128)(2,1)}, f32[512,1024]{1,0:T(8,128)}, bf16[512,1024]{1,0:T(8,128)(2,1)}, bf16[512,1024]{1,0:T(8,128)(2,1)}) custom-call(f32[4,9]{1,0:T(4,128)} %fusion.5.refs_0_, bf16[512,4096]{1,0:T(8,128)(2,1)} %refs_1_.7, bf16[512,4096]{1,0:T(8,128)(2,1)} %refs_2_.7, ...), custom_call_target="tpu_custom_call", output_to_operand_aliasing={{0}: (7, {})} | custom-call | flops 12079595520 | bytes 10485760 | tf_op jit(solution)/shard_map/attention_grads/pallas_call | solution.py:175
  168.8 22.0 %attention_grads.7 = (bf16[512,4096]{1,0:T(8,128)(2,1)}, f32[512,1024]{1,0:T(8,128)}, bf16[512,1024]{1,0:T(8,128)(2,1)}, bf16[512,1024]{1,0:T(8,128)(2,1)}) custom-call(f32[4,9]{1,0:T(4,128)} %fusion.5.refs_0_, bf16[512,4096]{1,0:T(8,128)(2,1)} %refs_1_.7, bf16[512,4096]{1,0:T(8,128)(2,1)} %refs_2_.7, ...), custom_call_target="tpu_custom_call", output_to_operand_aliasing={{0}: (7, {})} | custom-call | flops 12079595520 | bytes 10485760 | tf_op jit(solution)/shard_map/attention_grads/pallas_call | solution.py:175
  191.5 3.4 %collective-permute-start.15 = (bf16[512,1024]{1,0:T(8,128)(2,1)S(1)}, bf16[512,1024]{1,0:T(8,128)(2,1)S(1)}, u32[]{:S(2)}, u32[]{:S(2)}) collective-permute-start(bf16[512,1024]{1,0:T(8,128)(2,1)S(1)} %fusion.3), channel_id=1, source_target_pairs={{2,0},{3,1},{4,2},{5,3},{6,4},{7,5},{8,6},{9,7},{10,8},{11,9},{12,... | collective-permute-start | bytes 3145736 | tf_op jit(solution)/shard_map/ppermute | solution.py:25
  198.5 4.2 %collective-permute-start.11 = (bf16[512,1024]{1,0:T(8,128)(2,1)S(1)}, bf16[512,1024]{1,0:T(8,128)(2,1)}, u32[]{:S(2)}, u32[]{:S(2)}) collective-permute-start(bf16[512,1024]{1,0:T(8,128)(2,1)S(1)} %fusion.1), channel_id=1, source_target_pairs={{2,0},{3,1},{4,2},{5,3},{6,4},{7,5},{8,6},{9,7},{10,8},{11,9},{12,... | collective-permute-start | bytes 3145736 | tf_op jit(solution)/shard_map/ppermute | solution.py:25
  209.9 11.4 %collective-permute-done.15.refs_0_ = bf16[512,1024]{1,0:T(8,128)(2,1)S(1)} collective-permute-done((bf16[512,1024]{1,0:T(8,128)(2,1)S(1)}, bf16[512,1024]{1,0:T(8,128)(2,1)S(1)}, u32[]{:S(2)}, u32[]{:S(2)}) %collective-permute-start.15) | collective-permute-done | bytes 1048608 | tf_op jit(solution)/shard_map/ppermute | solution.py:25
  222.3 4.0 %sum_key_value_grads.4 = (bf16[512,2048]{1,0:T(8,128)(2,1)}, bf16[512,2048]{1,0:T(8,128)(2,1)}) custom-call(f32[512,1024]{1,0:T(8,128)} %get-tuple-element.40.own_ref, bf16[512,1024]{1,0:T(8,128)(2,1)} %copy-done.11, bf16[512,1024]{1,0:T(8,128)(2,1)} %broadcast_select_fusion.refs_1_), custom_call_target="tpu_custom_call" | custom-call | tf_op jit(solution)/shard_map/sum_key_value_grads/pallas_call | solution.py:225
  226.2 17.6 %collective-permute-done.13.refs_0_ = bf16[512,1024]{1,0:T(8,128)(2,1)} collective-permute-done((bf16[512,1024]{1,0:T(8,128)(2,1)S(1)}, bf16[512,1024]{1,0:T(8,128)(2,1)}, u32[]{:S(2)}, u32[]{:S(2)}) %collective-permute-start.13) | collective-permute-done | bytes 1048608 | tf_op jit(solution)/shard_map/ppermute | solution.py:25
  243.9 4.0 %sum_key_value_grads.5 = (bf16[512,2048]{1,0:T(8,128)(2,1)}, bf16[512,2048]{1,0:T(8,128)(2,1)}) custom-call(f32[512,1024]{1,0:T(8,128)} %get-tuple-element.37.own_ref, bf16[512,1024]{1,0:T(8,128)(2,1)} %collective-permute-done.13.refs_0_, bf16[512,1024]{1,0:T(8,128)(2,1)} %broadcast_select_fusion.1.refs_1_, ...), custom_call_target="tpu_custom_call", output_to_operand_aliasing={{0}: (3, {}), {1}: (4, {})} | custom-call | tf_op jit(solution)/shard_map/sum_key_value_grads/pallas_call | solution.py:225
  247.8 18.5 %collective-permute-done.11.refs_0_ = bf16[512,1024]{1,0:T(8,128)(2,1)} collective-permute-done((bf16[512,1024]{1,0:T(8,128)(2,1)S(1)}, bf16[512,1024]{1,0:T(8,128)(2,1)}, u32[]{:S(2)}, u32[]{:S(2)}) %collective-permute-start.11) | collective-permute-done | bytes 1048608 | tf_op jit(solution)/shard_map/ppermute | solution.py:25
  266.3 4.0 %sum_key_value_grads.6 = (bf16[512,2048]{1,0:T(8,128)(2,1)}, bf16[512,2048]{1,0:T(8,128)(2,1)}) custom-call(f32[512,1024]{1,0:T(8,128)} %get-tuple-element.34.own_ref, bf16[512,1024]{1,0:T(8,128)(2,1)} %collective-permute-done.11.refs_0_, bf16[512,1024]{1,0:T(8,128)(2,1)} %broadcast_select_fusion.2.refs_1_, ...), custom_call_target="tpu_custom_call", output_to_operand_aliasing={{0}: (3, {}), {1}: (4, {})} | custom-call | tf_op jit(solution)/shard_map/sum_key_value_grads/pallas_call | solution.py:225
  270.3 17.9 %collective-permute-done.9.refs_0_ = bf16[512,1024]{1,0:T(8,128)(2,1)} collective-permute-done((bf16[512,1024]{1,0:T(8,128)(2,1)S(1)}, bf16[512,1024]{1,0:T(8,128)(2,1)}, u32[]{:S(2)}, u32[]{:S(2)}) %collective-permute-start.9) | collective-permute-done | bytes 1048608 | tf_op jit(solution)/shard_map/ppermute | solution.py:25
  288.2 4.0 %sum_key_value_grads.7 = (bf16[512,2048]{1,0:T(8,128)(2,1)}, bf16[512,2048]{1,0:T(8,128)(2,1)}) custom-call(f32[512,1024]{1,0:T(8,128)} %get-tuple-element.31.own_ref, bf16[512,1024]{1,0:T(8,128)(2,1)} %collective-permute-done.9.refs_0_, bf16[512,1024]{1,0:T(8,128)(2,1)} %broadcast_select_fusion.3.refs_1_, ...), custom_call_target="tpu_custom_call", output_to_operand_aliasing={{0}: (3, {}), {1}: (4, {})} | custom-call | tf_op jit(solution)/shard_map/sum_key_value_grads/pallas_call | solution.py:225
  (66 shorter events, 24.9 us)
Async XLA Ops:
  0.6 27.9 %copy-start = (s32[128,9]{0,1:T(8,128)S(1)}, s32[128,9]{0,1:T(8,128)}, u32[]{:S(2)}) copy-start(s32[128,9]{0,1:T(8,128)} %param.9) | copy-start | bytes 13828
  4.2 28.2 %collective-permute-start.6 = (bf16[512,1024]{1,0:T(8,128)(2,1)}, bf16[512,1024]{1,0:T(8,128)(2,1)}, u32[]{:S(2)}, u32[]{:S(2)}) collective-permute-start(bf16[512,1024]{1,0:T(8,128)(2,1)} %pack_key_value.7), channel_id=1, source_target_pairs={{0,2},{1,3},{2,4},{3,5},{4,6},{5,7},{6,8},{7,9},{8,10},{9,11},{10,... | collective-permute-start | bytes 3145736 | tf_op jit(solution)/shard_map/ppermute | solution.py:25
  11.1 43.8 %collective-permute-start.4 = (bf16[512,1024]{1,0:T(8,128)(2,1)}, bf16[512,1024]{1,0:T(8,128)(2,1)}, u32[]{:S(2)}, u32[]{:S(2)}) collective-permute-start(bf16[512,1024]{1,0:T(8,128)(2,1)} %pack_key_value.6), channel_id=1, source_target_pairs={{0,2},{1,3},{2,4},{3,5},{4,6},{5,7},{6,8},{7,9},{8,10},{9,11},{10,... | collective-permute-start | bytes 3145736 | tf_op jit(solution)/shard_map/ppermute | solution.py:25
  18.0 14.4 %copy-start.5 = (bf16[512,1024]{1,0:T(8,128)(2,1)S(1)}, bf16[512,1024]{1,0:T(8,128)(2,1)}, u32[]{:S(2)}) copy-start(bf16[512,1024]{1,0:T(8,128)(2,1)} %pack_key_value.7) | copy-start | bytes 3145732
  18.0 59.4 %collective-permute-start.2 = (bf16[512,1024]{1,0:T(8,128)(2,1)}, bf16[512,1024]{1,0:T(8,128)(2,1)}, u32[]{:S(2)}, u32[]{:S(2)}) collective-permute-start(bf16[512,1024]{1,0:T(8,128)(2,1)} %pack_key_value.5), channel_id=1, source_target_pairs={{0,2},{1,3},{2,4},{3,5},{4,6},{5,7},{6,8},{7,9},{8,10},{9,11},{10,... | collective-permute-start | bytes 3145736 | tf_op jit(solution)/shard_map/ppermute | solution.py:25
  24.9 30.0 %copy-start.4 = (bf16[512,1024]{1,0:T(8,128)(2,1)S(1)}, bf16[512,1024]{1,0:T(8,128)(2,1)}, u32[]{:S(2)}) copy-start(bf16[512,1024]{1,0:T(8,128)(2,1)} %pack_key_value.6) | copy-start | bytes 3145732
  24.9 73.6 %collective-permute-start = (bf16[512,1024]{1,0:T(8,128)(2,1)}, bf16[512,1024]{1,0:T(8,128)(2,1)S(1)}, u32[]{:S(2)}, u32[]{:S(2)}) collective-permute-start(bf16[512,1024]{1,0:T(8,128)(2,1)} %pack_key_value.4), channel_id=1, source_target_pairs={{0,2},{1,3},{2,4},{3,5},{4,6},{5,7},{6,8},{7,9},{8,10},{9,11},{10,... | collective-permute-start | bytes 3145736 | tf_op jit(solution)/shard_map/ppermute | solution.py:25
  32.6 44.8 %copy-start.3 = (bf16[512,1024]{1,0:T(8,128)(2,1)S(1)}, bf16[512,1024]{1,0:T(8,128)(2,1)}, u32[]{:S(2)}) copy-start(bf16[512,1024]{1,0:T(8,128)(2,1)} %pack_key_value.5) | copy-start | bytes 3145732
  32.6 66.2 %collective-permute-start.7 = (bf16[512,1024]{1,0:T(8,128)(2,1)S(1)}, bf16[512,1024]{1,0:T(8,128)(2,1)S(1)}, u32[]{:S(2)}, u32[]{:S(2)}) collective-permute-start(bf16[512,1024]{1,0:T(8,128)(2,1)S(1)} %broadcast_select_fusion.4), channel_id=1, source_target_pairs={{0,1},{1,0},{2,3},{3,2},{4,5},{5,4},{6,7},{7,6},{8,9},{9,8},{10,11... | collective-permute-start | bytes 3145736 | tf_op jit(solution)/shard_map/ppermute | solution.py:30
  55.1 43.5 %copy-start.2 = (bf16[512,1024]{1,0:T(8,128)(2,1)S(1)}, bf16[512,1024]{1,0:T(8,128)(2,1)}, u32[]{:S(2)}) copy-start(bf16[512,1024]{1,0:T(8,128)(2,1)} %pack_key_value.4) | copy-start | bytes 3145732
  55.1 67.1 %collective-permute-start.5 = (bf16[512,1024]{1,0:T(8,128)(2,1)S(1)}, bf16[512,1024]{1,0:T(8,128)(2,1)}, u32[]{:S(2)}, u32[]{:S(2)}) collective-permute-start(bf16[512,1024]{1,0:T(8,128)(2,1)S(1)} %broadcast_select_fusion.5), channel_id=1, source_target_pairs={{0,1},{1,0},{2,3},{3,2},{4,5},{5,4},{6,7},{7,6},{8,9},{9,8},{10,11... | collective-permute-start | bytes 3145736 | tf_op jit(solution)/shard_map/ppermute | solution.py:30
  77.5 66.9 %collective-permute-start.3 = (bf16[512,1024]{1,0:T(8,128)(2,1)S(1)}, bf16[512,1024]{1,0:T(8,128)(2,1)S(1)}, u32[]{:S(2)}, u32[]{:S(2)}) collective-permute-start(bf16[512,1024]{1,0:T(8,128)(2,1)S(1)} %broadcast_select_fusion.6), channel_id=1, source_target_pairs={{0,1},{1,0},{2,3},{3,2},{4,5},{5,4},{6,7},{7,6},{8,9},{9,8},{10,11... | collective-permute-start | bytes 3145736 | tf_op jit(solution)/shard_map/ppermute | solution.py:30
  98.6 23.2 %copy-start.6 = (bf16[512,1024]{1,0:T(8,128)(2,1)}, bf16[512,1024]{1,0:T(8,128)(2,1)S(1)}, u32[]{:S(2)}) copy-start(bf16[512,1024]{1,0:T(8,128)(2,1)S(1)} %collective-permute-done.refs_5_) | copy-start | bytes 3145732
  98.7 69.1 %collective-permute-start.1 = (bf16[512,1024]{1,0:T(8,128)(2,1)S(1)}, bf16[512,1024]{1,0:T(8,128)(2,1)S(1)}, u32[]{:S(2)}, u32[]{:S(2)}) collective-permute-start(bf16[512,1024]{1,0:T(8,128)(2,1)S(1)} %broadcast_select_fusion.7), channel_id=1, source_target_pairs={{0,1},{1,0},{2,3},{3,2},{4,5},{5,4},{6,7},{7,6},{8,9},{9,8},{10,11... | collective-permute-start | bytes 3145736 | tf_op jit(solution)/shard_map/ppermute | solution.py:30
  121.8 69.3 %collective-permute-start.14 = (bf16[512,1024]{1,0:T(8,128)(2,1)}, bf16[512,1024]{1,0:T(8,128)(2,1)S(1)}, u32[]{:S(2)}, u32[]{:S(2)}) collective-permute-start(bf16[512,1024]{1,0:T(8,128)(2,1)} %get-tuple-element.42), channel_id=1, source_target_pairs={{0,1},{1,0},{2,3},{3,2},{4,5},{5,4},{6,7},{7,6},{8,9},{9,8},{10,11... | collective-permute-start | bytes 3145736 | tf_op jit(solution)/shard_map/ppermute | solution.py:30
  144.1 50.8 %collective-permute-start.12 = (bf16[512,1024]{1,0:T(8,128)(2,1)}, bf16[512,1024]{1,0:T(8,128)(2,1)S(1)}, u32[]{:S(2)}, u32[]{:S(2)}) collective-permute-start(bf16[512,1024]{1,0:T(8,128)(2,1)} %get-tuple-element.39), channel_id=1, source_target_pairs={{0,1},{1,0},{2,3},{3,2},{4,5},{5,4},{6,7},{7,6},{8,9},{9,8},{10,11... | collective-permute-start | bytes 3145736 | tf_op jit(solution)/shard_map/ppermute | solution.py:30
  167.4 30.6 %collective-permute-start.10 = (bf16[512,1024]{1,0:T(8,128)(2,1)}, bf16[512,1024]{1,0:T(8,128)(2,1)S(1)}, u32[]{:S(2)}, u32[]{:S(2)}) collective-permute-start(bf16[512,1024]{1,0:T(8,128)(2,1)} %get-tuple-element.36), channel_id=1, source_target_pairs={{0,1},{1,0},{2,3},{3,2},{4,5},{5,4},{6,7},{7,6},{8,9},{9,8},{10,11... | collective-permute-start | bytes 3145736 | tf_op jit(solution)/shard_map/ppermute | solution.py:30
  168.8 22.2 %copy-start.7 = (bf16[512,1024]{1,0:T(8,128)(2,1)S(1)}, bf16[512,1024]{1,0:T(8,128)(2,1)}, u32[]{:S(2)}) copy-start(bf16[512,1024]{1,0:T(8,128)(2,1)} %get-tuple-element.41) | copy-start | bytes 3145732
  190.8 11.9 %collective-permute-start.8 = (bf16[512,1024]{1,0:T(8,128)(2,1)}, bf16[512,1024]{1,0:T(8,128)(2,1)S(1)}, u32[]{:S(2)}, u32[]{:S(2)}) collective-permute-start(bf16[512,1024]{1,0:T(8,128)(2,1)} %get-tuple-element.33), channel_id=1, source_target_pairs={{0,1},{1,0},{2,3},{3,2},{4,5},{5,4},{6,7},{7,6},{8,9},{9,8},{10,11... | collective-permute-start | bytes 3145736 | tf_op jit(solution)/shard_map/ppermute | solution.py:30
  191.5 29.8 %collective-permute-start.15 = (bf16[512,1024]{1,0:T(8,128)(2,1)S(1)}, bf16[512,1024]{1,0:T(8,128)(2,1)S(1)}, u32[]{:S(2)}, u32[]{:S(2)}) collective-permute-start(bf16[512,1024]{1,0:T(8,128)(2,1)S(1)} %fusion.3), channel_id=1, source_target_pairs={{2,0},{3,1},{4,2},{5,3},{6,4},{7,5},{8,6},{9,7},{10,8},{11,9},{12,... | collective-permute-start | bytes 3145736 | tf_op jit(solution)/shard_map/ppermute | solution.py:25
  195.4 7.3 %copy-start.10 = (bf16[512,1024]{1,0:T(8,128)(2,1)S(1)}, bf16[512,1024]{1,0:T(8,128)(2,1)}, u32[]{:S(2)}) copy-start(bf16[512,1024]{1,0:T(8,128)(2,1)} %get-tuple-element.32) | copy-start | bytes 3145732
  195.4 48.5 %collective-permute-start.13 = (bf16[512,1024]{1,0:T(8,128)(2,1)S(1)}, bf16[512,1024]{1,0:T(8,128)(2,1)}, u32[]{:S(2)}, u32[]{:S(2)}) collective-permute-start(bf16[512,1024]{1,0:T(8,128)(2,1)S(1)} %fusion.2), channel_id=1, source_target_pairs={{2,0},{3,1},{4,2},{5,3},{6,4},{7,5},{8,6},{9,7},{10,8},{11,9},{12,... | collective-permute-start | bytes 3145736 | tf_op jit(solution)/shard_map/ppermute | solution.py:25
  198.5 67.8 %collective-permute-start.11 = (bf16[512,1024]{1,0:T(8,128)(2,1)S(1)}, bf16[512,1024]{1,0:T(8,128)(2,1)}, u32[]{:S(2)}, u32[]{:S(2)}) collective-permute-start(bf16[512,1024]{1,0:T(8,128)(2,1)S(1)} %fusion.1), channel_id=1, source_target_pairs={{2,0},{3,1},{4,2},{5,3},{6,4},{7,5},{8,6},{9,7},{10,8},{11,9},{12,... | collective-permute-start | bytes 3145736 | tf_op jit(solution)/shard_map/ppermute | solution.py:25
  203.2 85.1 %collective-permute-start.9 = (bf16[512,1024]{1,0:T(8,128)(2,1)S(1)}, bf16[512,1024]{1,0:T(8,128)(2,1)}, u32[]{:S(2)}, u32[]{:S(2)}) collective-permute-start(bf16[512,1024]{1,0:T(8,128)(2,1)S(1)} %fusion), channel_id=1, source_target_pairs={{2,0},{3,1},{4,2},{5,3},{6,4},{7,5},{8,6},{9,7},{10,8},{11,9},{12,... | collective-permute-start | bytes 3145736 | tf_op jit(solution)/shard_map/ppermute | solution.py:25
  (7 other events, 18.7 us)
